TPU v7x, 32 devices: a whole 2x2x4 slice. The times are simulated.
32 devices in a mesh: parts: 2 (over x), row: 16 (over z, y, core).
Axes of the slice: x: 2, y: 2, z: 4, core: 2. Of those that a mesh axis runs over, the one named last changes fastest.
Arguments:
- coords: int32 [4, 3, 512], P('parts'), parts along dimension 0, may hold values from 0 to 7
- labels: int32 [16, 16, 512], P('parts', 'row'), parts along dimension 0, may hold values from 0 to 255
- ranks: int32 [16, 16, 2], P('parts', 'row'), parts along dimension 0, may hold values from 16 to 128, as said below
- u_first: bfloat16 [16, 16, 512, 128], P('parts', 'row'), parts along dimension 0, may hold values from -6 to 6
- v_first: bfloat16 [16, 16, 512, 128], P('parts', 'row'), parts along dimension 0, may hold values from -0.0046875 to 0.0046875
- u_second: bfloat16 [16, 16, 512, 128], P('parts', 'row'), parts along dimension 0, may hold values from -6 to 6
- v_second: bfloat16 [16, 16, 512, 128], P('parts', 'row'), parts along dimension 0, may hold values from -0.01171875 to 0.01171875
Outputs:
- eliminated: float32 [16, 16, 512, 256], P('parts', 'row'), parts along dimension 0
- diagonal_factors: float32 [4, 512, 512], P('parts'), parts along dimension 0
There are 2 independent parts, one for each index of `parts`. A program takes and returns all parts, laid end to end along the dimension named above; each array names one. Nothing has to cross between parts.
Inputs may be any that keep to these rules, and one draw needn't show every extreme that they name: `ranks`: the block of tile 1 in column 0 has rank 128; some block has rank 128 // 8.
All inputs are finite; a program needn't handle non-finite values.
Results may differ from a plain program's by a relative error of at most 0.0003.
Values may be sent and summed in bfloat16 or wider, within the bound.
A program may use at most 128 MiB of HBM per device.

v0:
```python
import math

import jax
import jax.numpy as jnp
from jax import lax
from jax.sharding import PartitionSpec as P

NRHS = 256


highest = lax.Precision.HIGHEST
four_pi = 4.0 * math.pi


def spread(shard, axis, root):
    mine = lax.axis_index(axis) == root
    return lax.psum(jnp.where(mine, shard, jnp.zeros_like(shard)), axis)


def matmul(left, right):
    return jnp.dot(left, right, precision=highest, preferred_element_type=jnp.float32)


def kernel_tile(points):
    spots = points.astype(jnp.float32)
    distance = jnp.zeros((spots.shape[1], spots.shape[1]), jnp.float32)
    for dimension in range(3):
        offset = spots[dimension][:, None] - spots[dimension][None, :]
        distance = distance + offset * offset
    return 1.0 / (four_pi * jnp.sqrt(distance + 1.0)) + jnp.eye(spots.shape[1], dtype=jnp.float32)


def onehot(label_row):
    return (label_row[..., None] == jnp.arange(NRHS, dtype=jnp.int32)).astype(jnp.float32)


def triangular(lower, target):
    return lax.linalg.triangular_solve(lower, target, left_side=True, lower=True)


def solve_stack(lower, stack):
    number, height, breadth = stack.shape
    flat = jnp.transpose(stack, (1, 0, 2)).reshape(height, number * breadth)
    solved = triangular(lower, flat)
    return jnp.transpose(solved.reshape(height, number, breadth), (1, 0, 2))


def rank_mask(rank_values, breadth):
    columns = jnp.arange(breadth, dtype=jnp.int32)
    return (columns[None, :] < rank_values[:, None]).astype(jnp.float32)


def second_panel(points, label_row, u_one, w_one, first_sol):
    inner_gram = matmul(w_one.T, w_one)
    diagonal_tile = kernel_tile(points) - matmul(matmul(u_one, inner_gram), u_one.T)
    lower = jnp.linalg.cholesky(diagonal_tile)
    target = onehot(label_row) - matmul(u_one, matmul(w_one.T, first_sol))
    return (lower, triangular(lower, target))


def update(
    w_tiles, first_sol, second_lower, second_sol, u_one, w_one, label_rows, rank_rows, u0, u1, v1
):
    breadth = u0.shape[-1]
    u_zero = u0.astype(jnp.float32)
    u_next = u1.astype(jnp.float32)
    v_next = v1.astype(jnp.float32) * rank_mask(rank_rows[:, 1], breadth)[:, None, :]
    first_weights = jnp.einsum("nbr,bc->nrc", w_tiles, first_sol, precision=highest)
    first_update = jnp.einsum("nbr,nrc->nbc", u_zero, first_weights, precision=highest)
    cross = jnp.einsum("br,nbs->nrs", w_one, w_tiles, precision=highest)
    mixed = -jnp.einsum("br,nrs->nbs", u_one, cross, precision=highest)
    factor = solve_stack(second_lower, jnp.concatenate([v_next, mixed], axis=-1))
    second_weights = jnp.einsum("nbk,bc->nkc", factor, second_sol, precision=highest)
    left_pair = jnp.concatenate([u_next, u_zero], axis=-1)
    second_update = jnp.einsum("nbk,nkc->nbc", left_pair, second_weights, precision=highest)
    return onehot(label_rows) - first_update - second_update


def local(coords, labels, ranks, u_first, v_first, u_second, v_second):
    position = lax.axis_index("row")
    label_rows = labels[:, 0]
    rank_rows = ranks[:, 0]
    u_zero = u_first[:, 0]
    v_zero = v_first[:, 0]
    height = u_zero.shape[1]
    breadth = u_zero.shape[2]
    w_tiles = None

    def first_factor():
        lower = jnp.linalg.cholesky(kernel_tile(coords[0]))
        return (lower, triangular(lower, onehot(label_rows[0])))

    def first_empty():
        return (jnp.zeros((height, height), jnp.float32), jnp.zeros((height, NRHS), jnp.float32))

    first_lower, first_sol = lax.cond(position == 0, first_factor, first_empty)
    first_lower, first_sol = (spread(first_lower, "row", 0), spread(first_sol, "row", 0))
    masked = v_zero.astype(jnp.float32) * rank_mask(rank_rows[:, 0], breadth)[:, None, :]
    w_tiles = solve_stack(first_lower, masked)

    def second_factor():
        u_pick = u_zero[0].astype(jnp.float32)
        w_pick = w_tiles[0]
        lower, solved = second_panel(coords[1], label_rows[0], u_pick, w_pick, first_sol)
        return (lower, solved, u_pick, w_pick)

    def second_empty():
        return (
            jnp.zeros((height, height), jnp.float32),
            jnp.zeros((height, NRHS), jnp.float32),
            jnp.zeros((height, breadth), jnp.float32),
            jnp.zeros((height, breadth), jnp.float32),
        )

    second_lower, second_sol, u_one, w_one = lax.cond(position == 1, second_factor, second_empty)
    second_lower, second_sol, u_one, w_one = (
        spread(second_lower, "row", 1),
        spread(second_sol, "row", 1),
        spread(u_one, "row", 1),
        spread(w_one, "row", 1),
    )
    updated = update(
        w_tiles,
        first_sol,
        second_lower,
        second_sol,
        u_one,
        w_one,
        label_rows,
        rank_rows,
        u_zero,
        u_second[:, 0],
        v_second[:, 0],
    )
    leading = jnp.where(position == 0, first_sol, jnp.where(position == 1, second_sol, updated[0]))
    updated = updated.at[0].set(leading)
    return (updated[:, None], jnp.stack([first_lower, second_lower]))


def solution(mesh):
    in_specs = (
        P("parts", None, None),
        P("parts", "row", None),
        P("parts", "row", None),
        P("parts", "row", None, None),
        P("parts", "row", None, None),
        P("parts", "row", None, None),
        P("parts", "row", None, None),
    )
    out_specs = (P("parts", "row", None, None), P("parts", None, None))
    return jax.shard_map(local, mesh=mesh, in_specs=in_specs, out_specs=out_specs, check_vma=False)
```

profile of v0, /device:TPU:0, one launch (start us, length us, event | category | flops | bytes accessed | tf_op | source)
XLA Modules:
  0.0 670.5 jit_solution(9478993667882919614)
XLA Ops:
  7.9 145.0 %conditional.2 = (f32[512,512]{1,0:T(8,128)S(1)}, f32[512,256]{0,1:T(8,128)}) conditional(s32[]{:T(128)} %convert_element_type.64, () %tuple.30, (s32[2,3,512]{2,0,1:T(2,128)}, s32[8,512]{1,0:T(8,128)S(1)}) %tuple.157), branch_computations={%region_0.0_spmd, %region_1.12_spmd} | conditional | flops 916293632 | bytes 19471616 | solution.py:96
  11.5 11.7 %cholesky.286 = f32[128,128]{1,0:T(8,128)S(1)} custom-call(f32[128,128]{1,0:T(8,128)S(1)} %cholesky.426), custom_call_target="Cholesky" | custom-call | tf_op jit(solution)/shard_map/cond/branch_1_fun/jit(cholesky)/cholesky | solution.py:90
  23.3 9.8 %custom-call.35 = f32[1,128,128]{1,2,0:T(8,128)S(1)} custom-call(f32[1,128,128]{2,1,0:T(8,128)S(1)} %get-tuple-element.160), custom_call_target="InvertDiagBlocksLowerTriangular" | custom-call | tf_op jit(solution)/shard_map/cond/branch_1_fun/jit(cholesky)/cholesky | solution.py:90
  33.9 12.0 %cholesky.305 = f32[128,128]{1,0:T(8,128)S(1)} custom-call(f32[128,128]{1,0:T(8,128)S(1)} %cholesky.430), custom_call_target="Cholesky" | custom-call | tf_op jit(solution)/shard_map/cond/branch_1_fun/jit(cholesky)/cholesky | solution.py:90
  47.9 9.8 %custom-call.36 = f32[1,128,128]{1,2,0:T(8,128)S(1)} custom-call(f32[1,128,128]{2,1,0:T(8,128)S(1)} %get-tuple-element.157), custom_call_target="InvertDiagBlocksLowerTriangular" | custom-call | tf_op jit(solution)/shard_map/cond/branch_1_fun/jit(cholesky)/cholesky | solution.py:90
  58.4 11.7 %cholesky.326 = f32[128,128]{1,0:T(8,128)S(1)} custom-call(f32[128,128]{1,0:T(8,128)S(1)} %cholesky.435), custom_call_target="Cholesky" | custom-call | tf_op jit(solution)/shard_map/cond/branch_1_fun/jit(cholesky)/cholesky | solution.py:90
  71.5 9.8 %custom-call.37 = f32[1,128,128]{1,2,0:T(8,128)S(1)} custom-call(f32[1,128,128]{2,1,0:T(8,128)S(1)} %get-tuple-element.154), custom_call_target="InvertDiagBlocksLowerTriangular" | custom-call | tf_op jit(solution)/shard_map/cond/branch_1_fun/jit(cholesky)/cholesky | solution.py:90
  81.9 11.7 %cholesky.343 = f32[128,128]{1,0:T(8,128)S(1)} custom-call(f32[128,128]{1,0:T(8,128)S(1)} %convolution_subtract_fusion.5), custom_call_target="Cholesky" | custom-call | tf_op jit(solution)/shard_map/cond/branch_1_fun/jit(cholesky)/cholesky | solution.py:90
  95.3 10.6 %while.7 = (s32[]{:T(128)}, f32[512,512]{1,0:T(8,128)S(1)}, s32[4,2]{0,1:T(2,128)S(1)}, f32[4,128,128]{2,1,0:T(8,128)}, s32[]{:T(128)}) while((s32[]{:T(128)}, f32[512,512]{1,0:T(8,128)S(1)}, s32[4,2]{0,1:T(2,128)S(1)}, f32[4,128,128]{2,1,0:T(8,128)}, s32[]{:T(128)}) %tuple.135), condition=%wide.while_cond.1, body=%wide.while_body.1.sunk | while | flops 2 | bytes 132205 | solution.py:38
  95.9 2.0 bitcast_dynamic-update-slice_fusion.11
  98.6 2.0 bitcast_dynamic-update-slice_fusion.11
  101.2 2.0 bitcast_dynamic-update-slice_fusion.11
  103.8 2.0 bitcast_dynamic-update-slice_fusion.11
  105.8 40.1 %custom-call.38 = f32[4,128,128]{1,2,0:T(8,128)S(1)} custom-call(f32[4,128,128]{2,1,0:T(8,128)} %get-tuple-element.79), custom_call_target="InvertDiagBlocksLowerTriangular" | custom-call | tf_op jit(solution)/shard_map/cond/branch_1_fun/triangular_solve/custom-call.3 | solution.py:38
  145.9 1.2 fusion.17
  147.2 1.2 convolution_subtract_fusion.4
  148.6 1.2 convolution_subtract_fusion.2
  150.2 1.3 convolution_subtract_fusion.1
  151.8 1.0 copy.41
  153.0 1.1 broadcast_select_fusion.1
  154.1 1.9 broadcast_select_fusion.3
  156.9 1.1 fusion.143
  158.0 92.5 %all-reduce.8.cloned.1.call-done = (f32[512,256]{0,1:T(8,128)}, f32[512,512]{1,0:T(8,128)}) async-done(((f32[512,256]{0,1:T(8,128)}, f32[512,512]{1,0:T(8,128)}), (f32[512,256]{0,1:T(8,128)}, f32[512,512]{1,0:T(8,128)})) %all-reduce.8.cloned.1.call-update) | async-done | bytes 1572880 | tf_op jit(solution)/shard_map/psum | solution.py:17
  250.5 1.3 fusion.103
  251.9 8.0 %while.9 = (s32[]{:T(128)}, f32[512,512]{1,0:T(8,128)S(1)}, s32[4,2]{0,1:T(2,128)S(1)}, f32[4,128,128]{2,1,0:T(8,128)S(1)}, s32[]{:T(128)}) while((s32[]{:T(128)}, f32[512,512]{1,0:T(8,128)S(1)}, s32[4,2]{0,1:T(2,128)S(1)}, f32[4,128,128]{2,1,0:T(8,128)S(1)}, s32[]{:T(128)}) %tuple.140), condition=%wide.while_cond.2, body=%wide.while_body.2.sunk | while | flops 2 | bytes 131189 | solution.py:38
  252.5 1.4 bitcast_dynamic-update-slice_fusion.8
  254.5 1.4 bitcast_dynamic-update-slice_fusion.8
  256.5 1.4 bitcast_dynamic-update-slice_fusion.8
  258.5 1.4 bitcast_dynamic-update-slice_fusion.8
  259.9 39.3 %custom-call.29 = f32[4,128,128]{1,2,0:T(8,128)S(1)} custom-call(f32[4,128,128]{2,1,0:T(8,128)S(1)} %get-tuple-element.64), custom_call_target="InvertDiagBlocksLowerTriangular" | custom-call | tf_op jit(solution)/shard_map/triangular_solve | solution.py:38
  299.9 1.0 convolution_subtract_fusion.16
  301.5 1.8 convolution_subtract_fusion.15
  304.0 2.7 fusion.96
  307.4 1.5 bitcast_bitcast_fusion
  309.7 10.4 %conditional.3 = (f32[512,512]{1,0:T(8,128)}, f32[512,128]{1,0:T(8,128)}, f32[512,128]{1,0:T(8,128)S(1)}, f32[512,256]{0,1:T(8,128)}) conditional(s32[]{:T(128)} %convert_element_type.69, () %tuple.32, (s32[2,3,512]{2,0,1:T(2,128)S(1)}, f32[8,512,128]{2,1,0:T(8,128)}, bf16[8,512,128]{2,1,0:T(8,128)(2,1)S(1)}, s32[8,512]{1,0:T(8,128)S(1)}, ...), branch_computations={%region_12.15_spmd, %region_13.16_spmd} | conditional | flops 1919715328 | bytes 30088544 | solution.py:115
  311.3 1.1 broadcast.230
  320.1 1.1 broadcast_select_fusion
  323.0 1.3 copy.31
  324.3 1.5 convert_multiply_fusion
  326.0 2.0 fusion.109
  328.0 3.8 fusion.134
  331.8 234.4 %all-reduce.6.cloned.1.call-done = (f32[512,128]{1,0:T(8,128)}, f32[512,128]{1,0:T(8,128)}, f32[512,512]{1,0:T(8,128)}, f32[512,256]{0,1:T(8,128)}) async-done(((f32[512,128]{1,0:T(8,128)}, f32[512,128]{1,0:T(8,128)}, f32[512,512]{1,0:T(8,128)}, f32[512,256]{0,1:T(8,128)}), (f32[512,128]{1,0:T(8,128)}, f32[512,128]{1,0:T(8,128)}, f32[512,512]{1,0:T(8,128)}, ...) | async-done | bytes 2097168 | tf_op jit(solution)/shard_map/psum | solution.py:17
  566.3 5.6 convolution_bitcast_fusion.1
  572.0 8.2 %while.10 = (s32[]{:T(128)}, f32[512,512]{1,0:T(8,128)S(1)}, s32[4,2]{0,1:T(2,128)S(1)}, f32[4,128,128]{2,1,0:T(8,128)S(1)}, s32[]{:T(128)}) while((s32[]{:T(128)}, f32[512,512]{1,0:T(8,128)S(1)}, s32[4,2]{0,1:T(2,128)S(1)}, f32[4,128,128]{2,1,0:T(8,128)S(1)}, s32[]{:T(128)}) %tuple.156), condition=%wide.while_cond.3, body=%wide.while_body.3.sunk | while | flops 2 | bytes 131189 | solution.py:38
  572.7 1.4 bitcast_dynamic-update-slice_fusion.9
  574.8 1.4 bitcast_dynamic-update-slice_fusion.9
  576.8 1.4 bitcast_dynamic-update-slice_fusion.9
  578.9 1.4 bitcast_dynamic-update-slice_fusion.9
  580.9 40.3 %custom-call.30 = f32[4,128,128]{1,2,0:T(8,128)S(1)} custom-call(f32[4,128,128]{2,1,0:T(8,128)} %copy-done.22), custom_call_target="InvertDiagBlocksLowerTriangular" | custom-call | tf_op jit(solution)/shard_map/triangular_solve | solution.py:38
  621.2 2.9 negate_bitcast_fusion
  625.1 1.1 fusion.121
  626.2 1.8 convolution_subtract_fusion.14
  628.0 1.1 fusion.120
  629.1 3.5 convolution_subtract_fusion.13
  632.7 1.1 fusion.118
  633.7 5.5 fusion.80
  639.3 1.1 fusion.117
  640.9 2.0 copy.46
  642.9 7.8 %fusion.72 = f32[8,256,256]{2,1,0:T(8,128)S(1)} fusion(f32[8,512,256]{2,0,1:T(8,128)S(1)} %bitcast.272, f32[512,256]{0,1:T(8,128)S(1)} %copy-done.17), kind=kOutput, calls=%fused_computation.162 | convolution fusion | flops 3221225472 | bytes 6815744 | tf_op jit(solution)/shard_map/nbk,bc->nkc/dot_general | solution.py:73
  650.7 2.6 fusion.71
  653.3 1.9 copy.112
  655.3 0.9 fusion.107
  656.2 5.5 copy.35
  661.7 1.5 pad_maximum_fusion.3
  (128 shorter events, 27.6 us)
Async XLA Ops:
  7.2 243.3 %all-reduce.8.cloned.1.call-start = ((), (), s32[]{:S(2)}) async-start(), calls=%async_computation.1 | async-start | bytes 3145728 | tf_op jit(solution)/shard_map/psum | solution.py:17
  153.0 3.1 copy-start.24
  153.0 3.1 copy-start.20
  156.0 410.3 %all-reduce.6.cloned.1.call-start = ((), (), s32[]{:S(2)}) async-start(), calls=%async_computation | async-start | bytes 4194304 | tf_op jit(solution)/shard_map/psum | solution.py:17
  300.9 3.1 copy-start.18
  304.0 4.9 copy-start.6
  307.4 1.5 copy-start.15
  307.4 2.0 copy-start.3
  307.4 2.3 copy-start.12
  307.4 2.3 copy-start.23
  321.2 1.8 copy-start.21
  324.3 1.6 copy-start.7
  324.3 1.6 copy-start.13
  324.3 1.7 copy-start.16
  326.0 2.0 copy-start.4
  566.3 5.6 copy-start.9
  580.2 0.7 copy-start.22
  640.9 2.0 copy-start.17
  642.9 7.8 %copy-start = (f32[8,256,512]{2,1,0:T(8,128)S(1)}, f32[8,256,512]{2,1,0:T(8,128)}, u32[]{:S(2)}) copy-start(f32[8,256,512]{2,1,0:T(8,128)} %fusion.134) | copy-start | bytes 12582916
  642.9 7.8 %copy-start.5 = (bf16[8,1,512,128]{3,2,1,0:T(8,128)(2,1)S(1)}, bf16[8,1,512,128]{3,2,1,0:T(8,128)(2,1)}, u32[]{:S(2)}) copy-start(bf16[8,1,512,128]{3,2,1,0:T(8,128)(2,1)} %param.19) | copy-start | bytes 3145732
  642.9 7.8 %copy-start.19 = (bf16[8,1,512,128]{3,2,1,0:T(8,128)(2,1)S(1)}, bf16[8,1,512,128]{3,2,1,0:T(8,128)(2,1)}, u32[]{:S(2)}) copy-start(bf16[8,1,512,128]{3,2,1,0:T(8,128)(2,1)} %param.21) | copy-start | bytes 3145732
  653.3 2.0 copy-start.14
  656.2 5.5 copy-start.8
  656.2 5.5 copy-start.10
Sparse Core Ops, SparseCore 0:
  156.1 94.3 all-reduce.7
  323.0 243.1 all-reduce.5
where the time goes:
time: 680 us; the launch traced here: 670 us
  waiting for transfers between devices  327 us (48%)
  other arithmetic  215 us (32%)
  matrix products  55.6 us (8%)
  local copies, waits for them, and re-layouts  46.8 us (7%)
  between operations  15 us (2%)
  loops' own time  10.8 us (2%)
    psum x2, waiting for transfers between devices, spread(): return lax.psum(jnp.where(mine, shard, jnp.zeros_like(shard)), axis)  327 us
    another operation x11, other arithmetic, triangular(): lax.linalg.triangular_solve(lower, target, left_side=True, lower=True)  122 us
    another operation x14, other arithmetic, first_factor(): lower = jnp.linalg.cholesky(kernel_tile(coords[0]))  78.8 us
    another operation x21, matrix products, triangular(): lax.linalg.triangular_solve(lower, target, left_side=True, lower=True)  29 us
    another operation x29, local copies, waits for them, and re-layouts  19.5 us
    unnamed x52, local copies, waits for them, and re-layouts  13.7 us
  transfers between devices with their start and end apart: 2, of which 2 were waited for; matrix products, arithmetic and copies ran while one was open for 2% of the time, Pallas kernels for 0%

commit v1 on v0

v1 whole, which is shorter than its diff:
```python
import functools
import math

import jax
import jax.numpy as jnp
from jax import lax
from jax.experimental import pallas as pl
from jax.experimental.pallas import tpu as pltpu
from jax.sharding import PartitionSpec as P

NRHS = 256
NB = 128
RADIX = 8
F32 = jnp.float32
BF16 = jnp.bfloat16
four_pi = 4.0 * math.pi


def split(x):
    high = x.astype(BF16)
    return high, (x - high.astype(F32)).astype(BF16)


def dg(a, b, ca=1, cb=0):
    return lax.dot_general(a, b, (((ca,), (cb,)), ((), ())), preferred_element_type=F32)


def mm3(a, b, ca=1, cb=0):
    ah, al = split(a)
    bh, bl = split(b)
    return dg(ah, bh, ca, cb) + (dg(ah, bl, ca, cb) + dg(al, bh, ca, cb))


def mm_left(a, b, ca=1, cb=0):
    ah, al = split(a)
    return dg(ah, b, ca, cb) + dg(al, b, ca, cb)


def mm_right(a, b, ca=1, cb=0):
    bh, bl = split(b)
    return dg(a, bh, ca, cb) + dg(a, bl, ca, cb)


def columns_of(rows):
    pad = jnp.zeros((128 - rows.shape[0], rows.shape[1]), F32)
    return jnp.concatenate([rows, pad], axis=0).T


def kernel_tile(points):
    spots = points.astype(F32)
    n = spots.shape[1]
    cols = columns_of(spots)
    distance = jnp.zeros((n, n), F32)
    for dimension in range(3):
        offset = cols[:, dimension : dimension + 1] - spots[dimension : dimension + 1, :]
        distance = distance + offset * offset
    eye = eye_of(n)
    return lax.rsqrt(distance + 1.0) * (1.0 / four_pi) + eye


def eye_of(n):
    row = lax.broadcasted_iota(jnp.int32, (n, n), 0)
    col = lax.broadcasted_iota(jnp.int32, (n, n), 1)
    return jnp.where(row == col, 1.0, 0.0).astype(F32)


def onehot(label_column, dtype=F32):
    n = label_column.shape[0]
    lanes = lax.broadcasted_iota(jnp.int32, (n, NRHS), 1).astype(F32)
    return jnp.where(label_column == lanes, 1.0, 0.0).astype(dtype)


def sweep(blocks, out_refs):
    lane = lax.broadcasted_iota(jnp.int32, (1, NB), 1)
    active = list(blocks)
    for start in range(0, NB, RADIX):
        base = (start // 8) * 8
        off = start - base
        for which in range(len(active)):
            act = active[which]
            if off == 0 and start > 0:
                act = act[8:, :]
            cols = [
                jnp.broadcast_to(act[:, start + k : start + k + 1], act.shape) for k in range(RADIX)
            ]
            rows = [act[off + k : off + k + 1, :] for k in range(RADIX)]
            for k in range(RADIX):
                j = start + k
                pivot = cols[k][off + k : off + k + 1, :]
                root = lax.rsqrt(pivot)
                inverse = root * root
                scaled = jnp.where(lane == j, pivot + 1.0, rows[k]) * inverse
                final = jnp.where(lane < j, rows[k], jnp.where(lane == j, 1.0, 0.0)) * root
                out_refs[which][j : j + 1, :] = final
                for m in range(k + 1, RADIX):
                    entry = cols[k][off + m : off + m + 1, :]
                    rows[m] = rows[m] - entry * scaled
                    cols[m] = cols[m] - cols[k] * (entry * inverse)
                act = act - cols[k] * scaled
            active[which] = act


def factor(mats, inverses):
    height = mats[0].shape[0]
    steps = height // NB

    def step(b, carry):
        at = pl.ds(pl.multiple_of(b * NB, NB), NB)
        sweep([mat[at, at] for mat in mats], inverses)
        for s in range(steps):

            @pl.when(b == s)
            def _():
                lo, hi = s * NB, (s + 1) * NB
                for mat, inv in zip(mats, inverses):
                    panel = mm3(inv[...], mat[lo:hi, lo : height + hi])
                    mat[lo:hi, lo : height + hi] = panel
                    if hi < height:
                        left = panel[:, NB : height - lo]
                        mat[hi:, hi : height + hi] -= mm3(left, panel[:, NB:], 0, 0)

        return carry

    lax.fori_loop(0, steps, step, 0)


def triangle(upper):
    n = upper.shape[0]
    row = lax.broadcasted_iota(jnp.int32, (n, n), 0)
    col = lax.broadcasted_iota(jnp.int32, (n, n), 1)
    return jnp.where(row <= col, upper, 0.0)


def first_kernel(coords, mat, inverse):
    height = mat.shape[0]
    mat[:, :height] = kernel_tile(coords[0])
    mat[:, height:] = eye_of(height)
    factor([mat], [inverse])


def second_kernel(
    place, ranks, coords, labels, payload, first, u0, v0, u1, v1, out, diag,
    mat, inverse, lowers, heads, tails, lead, label_cols, sem,
):
    step = pl.program_id(0)
    height = mat.shape[0]
    rmax = u0.shape[-1]

    @pl.when(step == 0)
    def _():
        label_cols[...] = columns_of(labels[...].astype(F32))
        u_one = payload[:height, :rmax]
        v_one = payload[:height, rmax : 2 * rmax]
        marks = columns_of(payload[height : height + 16, :].astype(F32))
        b_zero = onehot(jnp.concatenate([marks[:, 0:1], marks[:, 1:2]], axis=0), BF16)
        b_one = onehot(jnp.concatenate([marks[:, 2:3], marks[:, 3:4]], axis=0))
        lower_inverse = first[:, height:]
        lowers[0] = triangle(first[:, :height]).T
        w_y = mm_left(lower_inverse, jnp.concatenate([v_one, b_zero], axis=1))
        gram = mm3(w_y[:, :rmax], w_y, 0, 0)
        spread = mm_right(u_one, gram)
        mat[:, :height] = kernel_tile(coords[1]) - mm_left(spread[:, :rmax], u_one, 1, 1)
        mat[:, height:] = eye_of(height)
        factor([mat], [inverse])
        second_inverse = mat[:, height:]
        y_one = mm3(second_inverse, b_one - spread[:, rmax:])
        lead[0] = w_y[:, rmax:]
        lead[1] = y_one
        lowers[1] = triangle(mat[:, :height]).T
        pltpu.make_async_copy(lowers, diag, sem).start()
        z_one = mm3(second_inverse, y_one, 0, 0)
        g_z = mm3(lower_inverse, w_y, 0, 0)
        blend = g_z[:, rmax:] - mm3(g_z[:, :rmax], mm_right(u_one, z_one, 0, 0))
        high, low = split(blend)
        heads[:, :NRHS] = high
        heads[:, NRHS:] = low
        high, low = split(z_one)
        tails[:, :NRHS] = high
        tails[:, NRHS:] = low

    lanes = lax.broadcasted_iota(jnp.int32, (height, rmax), 1)
    zero = jnp.zeros((), BF16)
    v_zero = jnp.where(lanes < ranks[step, 0], v0[0, 0], zero)
    v_next = jnp.where(lanes < ranks[step, 1], v1[0, 0], zero)
    m_zero = dg(v_zero, heads[...], 0, 0)
    m_next = dg(v_next, tails[...], 0, 0)
    weights = jnp.concatenate(
        [m_zero[:, :NRHS] + m_zero[:, NRHS:], m_next[:, :NRHS] + m_next[:, NRHS:]], axis=0
    )
    pair = jnp.concatenate([u0[0, 0], u1[0, 0]], axis=1)
    all_lanes = lax.broadcasted_iota(jnp.int32, label_cols.shape, 1)
    mark = jnp.sum(jnp.where(all_lanes == step, label_cols[...], 0.0), axis=1, keepdims=True)
    out[0, 0] = onehot(mark) - mm_right(pair, weights)

    @pl.when(jnp.logical_and(step == 0, place[0] < 2))
    def _():
        out[0, 0] = lead[place[0]]

    @pl.when(step == pl.num_programs(0) - 1)
    def _():
        pltpu.make_async_copy(lowers, diag, sem).wait()


def local(coords, labels, ranks, u_first, v_first, u_second, v_second):
    position = lax.axis_index("row")
    cycles, _, height, rmax = u_first.shape
    vmem = pltpu.CompilerParams(vmem_limit_bytes=56 * 1024 * 1024)
    zero = jnp.zeros((), BF16)
    keep = jnp.arange(rmax) < ranks[0, 0, 0]
    factors = jnp.concatenate(
        [u_first[0, 0], jnp.where(keep[None, :], v_first[0, 0], zero)], axis=1
    )
    mark = labels[0, 0].astype(BF16).reshape(height // NRHS, NRHS)
    mark_rows = jnp.concatenate(
        [
            jnp.where(position == 0, mark, zero),
            jnp.where(position == 1, mark, zero),
            jnp.zeros((16 - 2 * (height // NRHS), NRHS), BF16),
        ],
        axis=0,
    )
    payload = jnp.concatenate([jnp.where(position == 1, factors, zero), mark_rows], axis=0)
    payload = lax.psum(payload, "row")

    first = pl.pallas_call(
        first_kernel,
        out_shape=jax.ShapeDtypeStruct((height, 2 * height), F32),
        scratch_shapes=[pltpu.VMEM((NB, NB), F32)],
        compiler_params=vmem,
        cost_estimate=pl.CostEstimate(flops=40_000_000_000, bytes_accessed=2**21, transcendentals=0),
        name="first_factor",
    )(coords)

    tile = lambda width: pl.BlockSpec((1, 1, height, width), lambda i: (i, 0, 0, 0))
    whole = pl.BlockSpec(memory_space=pltpu.VMEM)
    smem = pl.BlockSpec(memory_space=pltpu.SMEM)
    updated, diag = pl.pallas_call(
        second_kernel,
        grid=(cycles,),
        out_shape=(
            jax.ShapeDtypeStruct((cycles, 1, height, NRHS), F32),
            jax.ShapeDtypeStruct((2, height, height), F32),
        ),
        in_specs=[smem, smem, whole, whole, whole, whole] + [tile(rmax)] * 4,
        out_specs=(tile(NRHS), pl.BlockSpec(memory_space=pl.ANY)),
        scratch_shapes=[
            pltpu.VMEM((height, 2 * height), F32),
            pltpu.VMEM((NB, NB), F32),
            pltpu.VMEM((2, height, height), F32),
            pltpu.VMEM((height, 2 * NRHS), BF16),
            pltpu.VMEM((height, 2 * NRHS), BF16),
            pltpu.VMEM((2, height, NRHS), F32),
            pltpu.VMEM((height, 128), F32),
            pltpu.SemaphoreType.DMA,
        ],
        compiler_params=vmem,
        name="second_factor_and_tiles",
    )(
        position.reshape(1).astype(jnp.int32),
        ranks[:, 0],
        coords,
        labels[:, 0],
        payload,
        first,
        u_first,
        v_first,
        u_second,
        v_second,
    )
    return updated, diag


def solution(mesh):
    in_specs = (
        P("parts", None, None),
        P("parts", "row", None),
        P("parts", "row", None),
        P("parts", "row", None, None),
        P("parts", "row", None, None),
        P("parts", "row", None, None),
        P("parts", "row", None, None),
    )
    out_specs = (P("parts", "row", None, None), P("parts", None, None))
    return jax.shard_map(local, mesh=mesh, in_specs=in_specs, out_specs=out_specs, check_vma=False)
```

time: 680 us -> 144 us (0.21); the launches traced: 670 us -> 143 us
  waiting for transfers between devices: 327 us -> 69.6 us
  other arithmetic: 215 us -> 3.17 us
  matrix products: 55.6 us -> 0 us
  Pallas kernels: 0 us -> 51.6 us
  local copies, waits for them, and re-layouts: 46.8 us -> 4.79 us
  loops' own time: 10.8 us -> 0 us
    psum x2 -> x1, waiting for transfers between devices: 327 us -> 69.6 us  [local(): payload = lax.psum(payload, 'row')]
    another operation x26 -> x0, other arithmetic: 202 us -> none  [the longest x11 122 us: triangular(): lax.linalg.triangular_solve(lower, target, left_side=True, lower=True)]
    pallas_call x0 -> x2, Pallas kernels: none -> 51.6 us  [the longest x1 32 us: local(): pl.pallas_call(second_kernel, grid=(cycles,), out_shape=(jax.ShapeDtypeSt...]
    another operation x49 -> x0, local copies, waits for them, and re-layouts: 31.8 us -> none
    another operation x27 -> x0, matrix products: 30.9 us -> none  [the longest x21 29 us: triangular(): lax.linalg.triangular_solve(lower, target, left_side=True, lower=True)]
    dot_general x6 -> x0, matrix products: 24.7 us -> none  [the longest x1 7.79 us: update(): jnp.einsum('nbk,bc->nkc', factor, second_sol, precision=highest)]
    unnamed x52 -> x6, local copies, waits for them, and re-layouts: 13.7 us -> 1.92 us
    another operation x5 -> x0, loops' own time: 10.8 us -> none  [the longest x1 7.71 us: local(): lax.cond(position == 1, second_factor, second_empty)]
  transfers between devices with their start and end apart: 2 -> 1, of which waited for: 2 -> 1; matrix products, arithmetic and copies ran while one was open for 2% -> 2% of each run, Pallas kernels for 0% -> 14%
where the time goes in v1:
time: 144 us; the launch traced here: 143 us
  waiting for transfers between devices  69.6 us (48%)
  Pallas kernels  51.6 us (36%)
  between operations  14.1 us (10%)
  local copies, waits for them, and re-layouts  4.79 us (3%)
  other arithmetic  3.17 us (2%)
    psum x1, waiting for transfers between devices, local(): payload = lax.psum(payload, 'row')  69.6 us
    pallas_call x1, Pallas kernels, local(): pl.pallas_call(second_kernel, grid=(cycles,), out_shape=(jax.ShapeDtypeSt...  32 us
    pallas_call x1, Pallas kernels, local(): pl.pallas_call(first_kernel, out_shape=jax.ShapeDtypeStruct((height, 2 *...  19.6 us
  transfers between devices with their start and end apart: 1, of which 1 were waited for; matrix products, arithmetic and copies ran while one was open for 2% of the time, Pallas kernels for 14%

profile of v1, /device:TPU:0, one launch (start us, length us, event | category | flops | bytes accessed | tf_op | source)
XLA Modules:
  0.0 143.3 jit_solution(3329158970572475120)
XLA Ops:
  7.2 0.0 all-reduce.2.cloned.1.call-start
  7.2 1.2 slice.14
  8.4 0.6 iota_compare_fusion
  9.1 0.7 fusion
  9.8 0.9 slice_bitcast_fusion
  10.7 0.1 pad.3.clone
  10.8 0.9 bitcast_select_fusion
  11.7 0.1 maximum_select_fusion
  11.8 0.8 maximum_maximum_fusion
  12.6 0.0 all-reduce.2.cloned.1.call-update
  12.7 1.3 copy.11.coords
  14.0 0.0 copy-start
  14.0 0.0 copy-start.1
  14.0 19.6 %first_factor.1.first = f32[512,1024]{1,0:T(8,128)} custom-call(s32[2,3,512]{2,1,0:T(4,128)} %copy.11.coords), custom_call_target="tpu_custom_call" | custom-call | flops 40000000000 | bytes 2097152 | tf_op jit(solution)/shard_map/first_factor/pallas_call | solution.py:225
  33.6 0.0 copy-done
  33.6 0.6 copy.14
  34.2 0.0 copy-done.1
  34.2 0.7 copy.10.ranks
  34.9 69.6 %all-reduce.2.cloned.1.call-done.payload = bf16[528,256]{1,0:T(8,128)(2,1)} async-done(((bf16[528,256]{1,0:T(8,128)(2,1)}), bf16[528,256]{1,0:T(8,128)(2,1)}) %all-reduce.2.cloned.1.call-update) | async-done | bytes 270352 | tf_op jit(solution)/shard_map/psum | solution.py:223
  104.5 32.0 %second_factor_and_tiles.1 = (f32[8,1,512,256]{3,2,1,0:T(8,128)}, f32[2,512,512]{2,1,0:T(8,128)}) custom-call(s32[1]{0:T(128)} %bitcast.place, s32[8,2]{1,0:T(8,128)} %copy.10.ranks, s32[2,3,512]{2,1,0:T(4,128)} %copy.11.coords, s32[8,512]{1,0:T(8,128)} %bitcast.10, bf16[528,256]{1,0:T(8,128)(2,1)} %all-reduce.2.cloned.1.call-done.payload, ...), custom_call_target="tpu_custom_call" | custom-call | tf_op jit(solution)/shard_map/second_factor_and_tiles/pallas_call | solution.py:237
  (3 shorter events, 0.0 us)
Async XLA Ops:
  7.2 97.3 %all-reduce.2.cloned.1.call-start = ((), (), s32[]{:S(2)}) async-start(), calls=%async_computation | async-start | bytes 540672 | tf_op jit(solution)/shard_map/psum | solution.py:223
  14.0 19.6 %copy-start = (s32[8,1,512]{2,1,0:T(1,128)S(1)}, s32[8,1,512]{2,1,0:T(1,128)}, u32[]{:S(2)}) copy-start(s32[8,1,512]{2,1,0:T(1,128)} %param.8) | copy-start | bytes 49156
  14.0 20.2 %copy-start.1 = (s32[8,1,2]{0,2,1:T(2,128)S(1)}, s32[8,1,2]{0,2,1:T(2,128)}, u32[]{:S(2)}) copy-start(s32[8,1,2]{0,2,1:T(2,128)} %param.9) | copy-start | bytes 196
Sparse Core Ops, SparseCore 0:
  12.8 91.6 all-reduce.1

commit v2 on v1

--- a/solution.py
+++ b/solution.py
@@ -1,4 +1,3 @@
-import functools
 import math
 
 import jax
@@ -100,7 +99,7 @@
             active[which] = act
 
 
-def factor(mats, inverses):
+def factor(mats, inverses, after_first=None):
     height = mats[0].shape[0]
     steps = height // NB
 
@@ -119,6 +118,8 @@
                         left = panel[:, NB : height - lo]
                         mat[hi:, hi : height + hi] -= mm3(left, panel[:, NB:], 0, 0)
 
+        if after_first is not None:
+            pl.when(b == 0)(after_first)
         return carry
 
     lax.fori_loop(0, steps, step, 0)
@@ -131,15 +132,122 @@
     return jnp.where(row <= col, upper, 0.0)
 
 
-def first_kernel(coords, mat, inverse):
+def first_kernel(
+    ranks, coords, labels, u_tile, v_tile, mat, pay_out, marks_out,
+    inverse, pay, marks, scatter_send, scatter_recv, gather_send, gather_recv, mark_send, mark_recv,
+):
+    me = lax.axis_index("row")
+    number = lax.axis_size("row")
     height = mat.shape[0]
+    rmax = pay.shape[1]
+    rows = pay.shape[0] // number
+    mesh_id = pl.DeviceIdType.MESH
+
+    def others(body):
+        def at(d, carry):
+            body(lax.rem(me + d, number))
+            return carry
+
+        lax.fori_loop(1, number, at, 0)
+
+    def piece(owner):
+        return pay.at[pl.ds(pl.multiple_of(owner * rows, rows), rows)]
+
+    def scatter(to):
+        return pltpu.make_async_remote_copy(
+            src_ref=piece(to), dst_ref=piece(to), send_sem=scatter_send.at[to],
+            recv_sem=scatter_recv, device_id={"row": to}, device_id_type=mesh_id,
+        )
+
+    def gather(owner, to):
+        return pltpu.make_async_remote_copy(
+            src_ref=piece(owner), dst_ref=piece(owner), send_sem=gather_send.at[to],
+            recv_sem=gather_recv.at[owner], device_id={"row": to}, device_id_type=mesh_id,
+        )
+
+    def mark(slot, to):
+        return pltpu.make_async_remote_copy(
+            src_ref=marks.at[slot], dst_ref=marks.at[slot], send_sem=mark_send.at[to],
+            recv_sem=mark_recv.at[slot], device_id={"row": to}, device_id_type=mesh_id,
+        )
+
+    barrier = pltpu.get_barrier_semaphore()
+    others(
+        lambda to: pl.semaphore_signal(
+            barrier, inc=1, device_id={"row": to}, device_id_type=mesh_id
+        )
+    )
+    for slot in range(2):
+
+        @pl.when(me == slot)
+        def _():
+            marks[slot] = labels[0:1, :]
+
+    @pl.when(me == 1)
+    def _():
+        lanes = lax.broadcasted_iota(jnp.int32, (height, rmax), 1)
+        pay[:height, :] = u_tile[0, 0]
+        pay[height:, :] = jnp.where(lanes < ranks[0, 0], v_tile[0, 0], jnp.zeros((), BF16))
+
+    pl.semaphore_wait(barrier, number - 1)
+
+    @pl.when(me == 1)
+    def _():
+        others(lambda to: scatter(to).start())
+
+    for slot in range(2):
+
+        @pl.when(me == slot)
+        def _():
+            others(lambda to: mark(slot, to).start())
+
     mat[:, :height] = kernel_tile(coords[0])
     mat[:, height:] = eye_of(height)
-    factor([mat], [inverse])
+
+    def pass_on():
+        @pl.when(me != 1)
+        def _():
+            scatter(me).wait_recv()
+
+        def send(to):
+            @pl.when(to != 1)
+            def _():
+                gather(me, to).start()
+
+        others(send)
+
+    factor([mat], [inverse], pass_on)
+
+    @pl.when(me != 1)
+    def _():
+        others(lambda owner: gather(owner, me).wait_recv())
+
+    @pl.when(me == 1)
+    def _():
+        others(lambda to: scatter(to).wait_send())
+
+    for slot in range(2):
+
+        @pl.when(me == slot)
+        def _():
+            others(lambda to: mark(slot, to).wait_send())
+
+        @pl.when(me != slot)
+        def _():
+            mark(slot, me).wait_recv()
+
+    def sent(to):
+        @pl.when(to != 1)
+        def _():
+            gather(me, to).wait_send()
+
+    others(sent)
+    pay_out[...] = pay[...]
+    marks_out[...] = marks[...]
 
 
 def second_kernel(
-    place, ranks, coords, labels, payload, first, u0, v0, u1, v1, out, diag,
+    place, ranks, coords, labels, payload, marks, first, u0, v0, u1, v1, out, diag,
     mat, inverse, lowers, heads, tails, lead, label_cols, sem,
 ):
     step = pl.program_id(0)
@@ -149,11 +257,11 @@
     @pl.when(step == 0)
     def _():
         label_cols[...] = columns_of(labels[...].astype(F32))
-        u_one = payload[:height, :rmax]
-        v_one = payload[:height, rmax : 2 * rmax]
-        marks = columns_of(payload[height : height + 16, :].astype(F32))
-        b_zero = onehot(jnp.concatenate([marks[:, 0:1], marks[:, 1:2]], axis=0), BF16)
-        b_one = onehot(jnp.concatenate([marks[:, 2:3], marks[:, 3:4]], axis=0))
+        u_one = payload[:height, :]
+        v_one = payload[height:, :]
+        marked = columns_of(jnp.concatenate([marks[0], marks[1]], axis=0).astype(F32))
+        b_zero = onehot(marked[:, 0:1], BF16)
+        b_one = onehot(marked[:, 1:2])
         lower_inverse = first[:, height:]
         lowers[0] = triangle(first[:, :height]).T
         w_y = mm_left(lower_inverse, jnp.concatenate([v_one, b_zero], axis=1))
@@ -205,35 +313,38 @@
     position = lax.axis_index("row")
     cycles, _, height, rmax = u_first.shape
     vmem = pltpu.CompilerParams(vmem_limit_bytes=56 * 1024 * 1024)
-    zero = jnp.zeros((), BF16)
-    keep = jnp.arange(rmax) < ranks[0, 0, 0]
-    factors = jnp.concatenate(
-        [u_first[0, 0], jnp.where(keep[None, :], v_first[0, 0], zero)], axis=1
-    )
-    mark = labels[0, 0].astype(BF16).reshape(height // NRHS, NRHS)
-    mark_rows = jnp.concatenate(
-        [
-            jnp.where(position == 0, mark, zero),
-            jnp.where(position == 1, mark, zero),
-            jnp.zeros((16 - 2 * (height // NRHS), NRHS), BF16),
-        ],
-        axis=0,
-    )
-    payload = jnp.concatenate([jnp.where(position == 1, factors, zero), mark_rows], axis=0)
-    payload = lax.psum(payload, "row")
-
-    first = pl.pallas_call(
-        first_kernel,
-        out_shape=jax.ShapeDtypeStruct((height, 2 * height), F32),
-        scratch_shapes=[pltpu.VMEM((NB, NB), F32)],
-        compiler_params=vmem,
-        cost_estimate=pl.CostEstimate(flops=40_000_000_000, bytes_accessed=2**21, transcendentals=0),
-        name="first_factor",
-    )(coords)
-
-    tile = lambda width: pl.BlockSpec((1, 1, height, width), lambda i: (i, 0, 0, 0))
+    number = lax.axis_size("row")
     whole = pl.BlockSpec(memory_space=pltpu.VMEM)
     smem = pl.BlockSpec(memory_space=pltpu.SMEM)
+    lead_tile = pl.BlockSpec((1, 1, height, rmax), lambda i: (0, 0, 0, 0))
+    first, payload, marks = pl.pallas_call(
+        first_kernel,
+        grid=(1,),
+        out_shape=(
+            jax.ShapeDtypeStruct((height, 2 * height), F32),
+            jax.ShapeDtypeStruct((2 * height, rmax), BF16),
+            jax.ShapeDtypeStruct((2, 1, height), jnp.int32),
+        ),
+        in_specs=[smem, whole, whole, lead_tile, lead_tile],
+        out_specs=(whole, whole, whole),
+        scratch_shapes=[
+            pltpu.VMEM((NB, NB), F32),
+            pltpu.VMEM((2 * height, rmax), BF16),
+            pltpu.VMEM((2, 1, height), jnp.int32),
+            pltpu.SemaphoreType.DMA((number,)),
+            pltpu.SemaphoreType.DMA,
+            pltpu.SemaphoreType.DMA((number,)),
+            pltpu.SemaphoreType.DMA((number,)),
+            pltpu.SemaphoreType.DMA((number,)),
+            pltpu.SemaphoreType.DMA((2,)),
+        ],
+        compiler_params=pltpu.CompilerParams(
+            vmem_limit_bytes=48 * 1024 * 1024, collective_id=0, has_side_effects=True
+        ),
+        name="first_factor_and_spread",
+    )(ranks[:, 0], coords, labels[:, 0], u_first, v_first)
+
+    tile = lambda width: pl.BlockSpec((1, 1, height, width), lambda i: (i, 0, 0, 0))
     updated, diag = pl.pallas_call(
         second_kernel,
         grid=(cycles,),
@@ -241,7 +352,7 @@
             jax.ShapeDtypeStruct((cycles, 1, height, NRHS), F32),
             jax.ShapeDtypeStruct((2, height, height), F32),
         ),
-        in_specs=[smem, smem, whole, whole, whole, whole] + [tile(rmax)] * 4,
+        in_specs=[smem, smem, whole, whole, whole, whole, whole] + [tile(rmax)] * 4,
         out_specs=(tile(NRHS), pl.BlockSpec(memory_space=pl.ANY)),
         scratch_shapes=[
             pltpu.VMEM((height, 2 * height), F32),
@@ -261,6 +372,7 @@
         coords,
         labels[:, 0],
         payload,
+        marks,
         first,
         u_first,
         v_first,

time: 144 us -> 66.4 us (0.46)
  waiting for transfers between devices: 69.6 us -> 0 us
  between operations: 14.1 us -> 0.82 us
  Pallas kernels: 51.6 us -> 57.8 us
  other arithmetic: 3.17 us -> 0 us
  local copies, waits for them, and re-layouts: 4.79 us -> 7.28 us
    psum x1 -> x0, waiting for transfers between devices: 69.6 us -> none  [local(): payload = lax.psum(payload, 'row')]
    pallas_call x1, Pallas kernels: 19.6 us -> 25.7 us  [local(): pl.pallas_call(first_kernel, grid=(1,), out_shape=(jax.ShapeDtypeStruct((...]
    unnamed x6 -> x18, local copies, waits for them, and re-layouts: 1.92 us -> 6.53 us
    select_n x3 -> x0, other arithmetic: 1.68 us -> none  [the longest x1 0.92 us: local(): jnp.where(keep[None, :], v_first[0, 0], zero)]
  transfers between devices with their start and end apart: 1 -> 0, of which waited for: 1 -> 0; matrix products, arithmetic and copies ran while one was open for 2% -> 0% of each run, Pallas kernels for 14% -> 0%
where the time goes in v2:
time: 66.4 us; the launch traced here: 65.9 us
  Pallas kernels  57.8 us (87%)
  local copies, waits for them, and re-layouts  7.28 us (11%)
  between operations  0.82 us (1%)
    pallas_call x1, Pallas kernels, local(): pl.pallas_call(second_kernel, grid=(cycles,), out_shape=(jax.ShapeDtypeSt...  32.1 us
    pallas_call x1, Pallas kernels, local(): pl.pallas_call(first_kernel, grid=(1,), out_shape=(jax.ShapeDtypeStruct((...  25.7 us
    unnamed x18, local copies, waits for them, and re-layouts  6.53 us

profile of v2, /device:TPU:0, one launch (start us, length us, event | category | flops | bytes accessed | tf_op | source)
XLA Modules:
  0.0 65.9 jit_solution(12252963078147664853)
XLA Ops:
  0.6 0.8 %copy.11.ranks = s32[8,2]{1,0:T(8,128)S(1)} copy(s32[8,2]{0,1:T(2,128)} %bitcast.7) | data formatting | bytes 128 | tf_op jit(solution)/shard_map/squeeze | solution.py:371
  1.4 0.0 copy-start.6
  1.4 0.7 %copy.12.coords = s32[2,3,512]{2,1,0:T(4,128)S(1)} copy(s32[2,3,512]{2,0,1:T(2,128)} %param.7) | data formatting | bytes 24576 | tf_op args[0]
  2.1 0.0 copy-start.4
  2.1 0.7 %copy.15 = s32[8,1,512]{2,0,1:T(8,128)S(1)} copy(s32[8,1,512]{2,1,0:T(1,128)} %param.8) | data formatting | bytes 32768
  2.8 0.0 copy-start.5
  2.8 0.0 copy-start
  2.8 1.2 %copy-done = bf16[8,1,512,128]{3,2,1,0:T(8,128)(2,1)S(1)} copy-done((bf16[8,1,512,128]{3,2,1,0:T(8,128)(2,1)S(1)}, bf16[8,1,512,128]{3,2,1,0:T(8,128)(2,1)}, u32[]{:S(2)}) %copy-start) | copy-done | bytes 1048600
  4.1 0.0 copy-start.1
  4.1 1.2 %copy-done.1 = bf16[8,1,512,128]{3,2,1,0:T(8,128)(2,1)S(1)} copy-done((bf16[8,1,512,128]{3,2,1,0:T(8,128)(2,1)S(1)}, bf16[8,1,512,128]{3,2,1,0:T(8,128)(2,1)}, u32[]{:S(2)}) %copy-start.1) | copy-done | bytes 1048600
  5.3 25.7 %first_factor_and_spread.1 = (f32[512,1024]{1,0:T(8,128)S(1)}, bf16[1024,128]{1,0:T(8,128)(2,1)S(1)}, s32[2,1,512]{2,1,0:T(1,128)S(1)}) custom-call(s32[8,2]{1,0:T(8,128)S(1)} %copy.11.ranks, s32[2,3,512]{2,1,0:T(4,128)S(1)} %copy.12.coords, s32[8,512]{1,0:T(8,128)S(1)} %bitcast.5, bf16[8,1,512,128]{3,2,1,0:T(8,128)(2,1)S(1)} %copy-done, ...), custom_call_target="tpu_custom_call" | custom-call | tf_op jit(solution)/shard_map/first_factor_and_spread/pallas_call | solution.py:320
  31.0 0.0 copy-start.2
  31.0 1.3 %copy-done.2 = f32[512,1024]{1,0:T(8,128)} copy-done((f32[512,1024]{1,0:T(8,128)}, f32[512,1024]{1,0:T(8,128)S(1)}, u32[]{:S(2)}) %copy-start.2) | copy-done | bytes 2097176
  32.3 0.0 copy-start.3
  32.3 0.7 %copy-done.3 = bf16[1024,128]{1,0:T(8,128)(2,1)} copy-done((bf16[1024,128]{1,0:T(8,128)(2,1)}, bf16[1024,128]{1,0:T(8,128)(2,1)S(1)}, u32[]{:S(2)}) %copy-start.3) | copy-done | bytes 262168
  33.0 0.0 copy-start.7
  33.0 0.6 copy-done.7
  33.6 0.0 copy-done.6
  33.6 0.0 copy-done.4
  33.6 0.0 copy-done.5
  33.6 32.1 %second_factor_and_tiles.1 = (f32[8,1,512,256]{3,2,1,0:T(8,128)}, f32[2,512,512]{2,1,0:T(8,128)}) custom-call(s32[1]{0:T(128)} %bitcast.place, s32[8,2]{1,0:T(8,128)} %copy-done.6, s32[2,3,512]{2,1,0:T(4,128)} %copy-done.4, s32[8,512]{1,0:T(8,128)} %bitcast.6, bf16[1024,128]{1,0:T(8,128)(2,1)} %copy-done.3, s32[2,1,512]{2,1,0:T(1,128)} %copy-done.7, ...), custom_call_target="tpu_custom_call" | custom-call | tf_op jit(solution)/shard_map/second_factor_and_tiles/pallas_call | solution.py:348
Async XLA Ops:
  1.4 32.2 %copy-start.6 = (s32[8,2]{1,0:T(8,128)}, s32[8,2]{1,0:T(8,128)S(1)}, u32[]{:S(2)}) copy-start(s32[8,2]{1,0:T(8,128)S(1)} %copy.11.ranks) | copy-start | bytes 196
  2.1 31.5 %copy-start.4 = (s32[2,3,512]{2,1,0:T(4,128)}, s32[2,3,512]{2,1,0:T(4,128)S(1)}, u32[]{:S(2)}) copy-start(s32[2,3,512]{2,1,0:T(4,128)S(1)} %copy.12.coords) | copy-start | bytes 36868
  2.8 30.8 %copy-start.5 = (s32[8,1,512]{2,0,1:T(8,128)}, s32[8,1,512]{2,0,1:T(8,128)S(1)}, u32[]{:S(2)}) copy-start(s32[8,1,512]{2,0,1:T(8,128)S(1)} %copy.15) | copy-start | bytes 49156
  2.8 1.2 %copy-start = (bf16[8,1,512,128]{3,2,1,0:T(8,128)(2,1)S(1)}, bf16[8,1,512,128]{3,2,1,0:T(8,128)(2,1)}, u32[]{:S(2)}) copy-start(bf16[8,1,512,128]{3,2,1,0:T(8,128)(2,1)} %u0.1) | copy-start | bytes 3145732
  4.1 1.2 %copy-start.1 = (bf16[8,1,512,128]{3,2,1,0:T(8,128)(2,1)S(1)}, bf16[8,1,512,128]{3,2,1,0:T(8,128)(2,1)}, u32[]{:S(2)}) copy-start(bf16[8,1,512,128]{3,2,1,0:T(8,128)(2,1)} %v0.1) | copy-start | bytes 3145732
  31.0 1.3 %copy-start.2 = (f32[512,1024]{1,0:T(8,128)}, f32[512,1024]{1,0:T(8,128)S(1)}, u32[]{:S(2)}) copy-start(f32[512,1024]{1,0:T(8,128)S(1)} %get-tuple-element.7.first) | copy-start | bytes 6291460
  32.3 0.7 %copy-start.3 = (bf16[1024,128]{1,0:T(8,128)(2,1)}, bf16[1024,128]{1,0:T(8,128)(2,1)S(1)}, u32[]{:S(2)}) copy-start(bf16[1024,128]{1,0:T(8,128)(2,1)S(1)} %get-tuple-element.5.payload) | copy-start | bytes 786436
  33.0 0.6 copy-start.7

commit v3 on v2

v3 whole, which is shorter than its diff:
```python
import math

import jax
import jax.numpy as jnp
from jax import lax
from jax.experimental import pallas as pl
from jax.experimental.pallas import tpu as pltpu
from jax.sharding import PartitionSpec as P

NRHS = 256
NB = 128
RADIX = 4
VMEM_BYTES = 60 * 1024 * 1024
F32 = jnp.float32
BF16 = jnp.bfloat16
four_pi = 4.0 * math.pi


def split(x):
    high = x.astype(BF16)
    return high, (x - high.astype(F32)).astype(BF16)


def dg(a, b, ca=1, cb=0):
    return lax.dot_general(a, b, (((ca,), (cb,)), ((), ())), preferred_element_type=F32)


def mm3(a, b, ca=1, cb=0):
    ah, al = split(a)
    bh, bl = split(b)
    return dg(ah, bh, ca, cb) + (dg(ah, bl, ca, cb) + dg(al, bh, ca, cb))


def mm_left(a, b, ca=1, cb=0):
    ah, al = split(a)
    return dg(ah, b, ca, cb) + dg(al, b, ca, cb)


def mm_right(a, b, ca=1, cb=0):
    bh, bl = split(b)
    return dg(a, bh, ca, cb) + dg(a, bl, ca, cb)


def columns_of(rows):
    pad = jnp.zeros((128 - rows.shape[0], rows.shape[1]), F32)
    return jnp.concatenate([rows, pad], axis=0).T


def kernel_tile(points):
    spots = points.astype(F32)
    n = spots.shape[1]
    cols = columns_of(spots)
    distance = jnp.zeros((n, n), F32)
    for dimension in range(3):
        offset = cols[:, dimension : dimension + 1] - spots[dimension : dimension + 1, :]
        distance = distance + offset * offset
    eye = eye_of(n)
    return lax.rsqrt(distance + 1.0) * (1.0 / four_pi) + eye


def eye_of(n):
    row = lax.broadcasted_iota(jnp.int32, (n, n), 0)
    col = lax.broadcasted_iota(jnp.int32, (n, n), 1)
    return jnp.where(row == col, 1.0, 0.0).astype(F32)


def onehot(label_column, dtype=F32):
    n = label_column.shape[0]
    lanes = lax.broadcasted_iota(jnp.int32, (n, NRHS), 1).astype(F32)
    return jnp.where(label_column == lanes, 1.0, 0.0).astype(dtype)


def sweep(blocks, out_refs):
    lane = lax.broadcasted_iota(jnp.int32, (1, NB), 1)
    active = list(blocks)
    every = range(len(active))
    for start in range(0, NB, RADIX):
        off = start % 8
        if off == 0 and start > 0:
            active = [act[8:, :] for act in active]
        cols = [
            [jnp.broadcast_to(act[:, start + k : start + k + 1], act.shape) for k in range(RADIX)]
            for act in active
        ]
        rows = [[act[off + k : off + k + 1, :] for k in range(RADIX)] for act in active]
        for k in range(RADIX):
            j = start + k
            for w in every:
                pivot = cols[w][k][off + k : off + k + 1, :]
                root = lax.rsqrt(pivot)
                inverse = root * root
                scaled = jnp.where(lane == j, pivot + 1.0, rows[w][k]) * inverse
                final = jnp.where(lane < j, rows[w][k], jnp.where(lane == j, 1.0, 0.0)) * root
                out_refs[w][j : j + 1, :] = final
                for m in range(k + 1, RADIX):
                    entry = cols[w][k][off + m : off + m + 1, :]
                    rows[w][m] = rows[w][m] - entry * scaled
                    cols[w][m] = cols[w][m] - cols[w][k] * (entry * inverse)
                active[w] = active[w] - cols[w][k] * scaled


def factor(mats, inverses):
    height = mats[0].shape[0]
    steps = height // NB

    def step(b, carry):
        at = pl.ds(pl.multiple_of(b * NB, NB), NB)
        sweep([mat[at, at] for mat in mats], inverses)
        for s in range(steps):

            @pl.when(b == s)
            def _():
                lo, hi = s * NB, (s + 1) * NB
                for mat, inv in zip(mats, inverses):
                    panel = mm3(inv[...], mat[lo:hi, lo : height + hi])
                    mat[lo:hi, lo : height + hi] = panel
                    if hi < height:
                        left = panel[:, NB : height - lo]
                        mat[hi:, hi : height + hi] -= mm3(left, panel[:, NB:], 0, 0)

        return carry

    lax.fori_loop(0, steps, step, 0)


def near_inverse(tile):
    n = tile.shape[0]
    top = 1.0 + n / four_pi
    rho = (top - 1.0) / (top + 1.0)
    scale = 2.0 / (1.0 + top)
    gain = 2.0 / (2.0 - rho * rho)
    inverse = (gain * scale) * (2.0 * eye_of(n) - scale * tile)
    rho = rho * rho / (2.0 - rho * rho)
    narrow = tile.astype(BF16)
    while rho > 0.05:
        gain = 2.0 / (2.0 - rho * rho)
        flat = inverse.astype(BF16)
        product = dg(narrow, flat).astype(BF16)
        inverse = gain * (2.0 * inverse - dg(flat, product))
        rho = rho * rho / (2.0 - rho * rho)
    return inverse


def refined(tile, inverse, target):
    flat = inverse.astype(BF16)
    solved = dg(flat, target.astype(BF16))
    for _ in range(6):
        solved = solved + dg(flat, (target - mm3(tile, solved)).astype(BF16))
    return solved


def triangle(upper):
    n = upper.shape[0]
    row = lax.broadcasted_iota(jnp.int32, (n, n), 0)
    col = lax.broadcasted_iota(jnp.int32, (n, n), 1)
    return jnp.where(row <= col, upper, 0.0)


def first_kernel(
    ranks, coords, labels, u_tile, v_tile, heads, tails, lead, lowers,
    mat_zero, mat_one, part_zero, part_one, pay, marks, scatter_send, scatter_recv, gather_send, gather_recv, mark_send, mark_recv,
):
    me = lax.axis_index("row")
    number = lax.axis_size("row")
    height = mat_zero.shape[0]
    rmax = pay.shape[1]
    rows = pay.shape[0] // number
    mesh_id = pl.DeviceIdType.MESH

    def others(body):
        def at(d, carry):
            body(lax.rem(me + d, number))
            return carry

        lax.fori_loop(1, number, at, 0)

    def piece(owner):
        return pay.at[pl.ds(pl.multiple_of(owner * rows, rows), rows)]

    def scatter(to):
        return pltpu.make_async_remote_copy(
            src_ref=piece(to), dst_ref=piece(to), send_sem=scatter_send.at[to],
            recv_sem=scatter_recv, device_id={"row": to}, device_id_type=mesh_id,
        )

    def gather(owner, to):
        return pltpu.make_async_remote_copy(
            src_ref=piece(owner), dst_ref=piece(owner), send_sem=gather_send.at[to],
            recv_sem=gather_recv.at[owner], device_id={"row": to}, device_id_type=mesh_id,
        )

    def mark(slot, to):
        return pltpu.make_async_remote_copy(
            src_ref=marks.at[slot], dst_ref=marks.at[slot], send_sem=mark_send.at[to],
            recv_sem=mark_recv.at[slot], device_id={"row": to}, device_id_type=mesh_id,
        )

    barrier = pltpu.get_barrier_semaphore()
    others(
        lambda to: pl.semaphore_signal(
            barrier, inc=1, device_id={"row": to}, device_id_type=mesh_id
        )
    )
    for slot in range(2):

        @pl.when(me == slot)
        def _():
            marks[slot] = labels[0]

    @pl.when(me == 1)
    def _():
        lanes = lax.broadcasted_iota(jnp.int32, (height, rmax), 1)
        pay[:height, :] = u_tile[0, 0]
        pay[height:, :] = jnp.where(lanes < ranks[0, 0, 0], v_tile[0, 0], jnp.zeros((), BF16))

    pl.semaphore_wait(barrier, number - 1)

    @pl.when(me == 1)
    def _():
        others(lambda to: scatter(to).start())

    for slot in range(2):

        @pl.when(me == slot)
        def _():
            others(lambda to: mark(slot, to).start())

    tile_zero = kernel_tile(coords[0])
    mat_zero[:, :height] = tile_zero
    mat_zero[:, height:] = eye_of(height)
    inverse = near_inverse(tile_zero)

    @pl.when(me != 1)
    def _():
        scatter(me).wait_recv()

    def send(to):
        @pl.when(to != 1)
        def _():
            gather(me, to).start()

    others(send)
    mat_one[:, :height] = kernel_tile(coords[1])
    mat_one[:, height:] = eye_of(height)

    @pl.when(me != 1)
    def _():
        others(lambda owner: gather(owner, me).wait_recv())

    @pl.when(me == 1)
    def _():
        others(lambda to: scatter(to).wait_send())

    for slot in range(2):

        @pl.when(me == slot)
        def _():
            others(lambda to: mark(slot, to).wait_send())

        @pl.when(me != slot)
        def _():
            mark(slot, me).wait_recv()

    def sent(to):
        @pl.when(to != 1)
        def _():
            gather(me, to).wait_send()

    others(sent)
    u_one = pay[:height, :]
    v_one = pay[height:, :]
    marked = columns_of(jnp.concatenate([marks[0], marks[1]], axis=0).astype(F32))
    b_zero = onehot(marked[:, 0:1], BF16)
    b_one = onehot(marked[:, 1:2])
    solved = refined(tile_zero, inverse, v_one.astype(F32))
    both = jnp.concatenate([v_one, b_zero], axis=1)
    spread = mm_right(u_one, mm_left(solved, both, 0, 0))
    mat_one[:, :height] -= mm_left(spread[:, :rmax], u_one, 1, 1)
    factor([mat_zero, mat_one], [part_zero, part_one])
    y_zero = mm_left(mat_zero[:, height:], b_zero)
    y_one = mm3(mat_one[:, height:], b_one - spread[:, rmax:])
    lead[0] = y_zero
    lead[1] = y_one
    lowers[0] = triangle(mat_zero[:, :height]).T
    lowers[1] = triangle(mat_one[:, :height]).T
    z_one = mm3(mat_one[:, height:], y_one, 0, 0)
    z_zero = mm3(mat_zero[:, height:], y_zero, 0, 0)
    blend = z_zero - mm3(solved, mm_right(u_one, z_one, 0, 0))
    high, low = split(blend)
    heads[:, :NRHS] = high
    heads[:, NRHS:] = low
    high, low = split(z_one)
    tails[:, :NRHS] = high
    tails[:, NRHS:] = low


def second_kernel(
    place, ranks, labels, heads, tails, lead, lowers, u0, v0, u1, v1, out, diag, label_cols, sem
):
    step = pl.program_id(0)
    height, rmax = u0.shape[2:]

    @pl.when(step == 0)
    def _():
        pltpu.make_async_copy(lowers, diag, sem).start()
        rows = [labels[i] for i in range(labels.shape[0])]
        label_cols[...] = columns_of(jnp.concatenate(rows, axis=0).astype(F32))

    lanes = lax.broadcasted_iota(jnp.int32, (height, rmax), 1)
    zero = jnp.zeros((), BF16)
    v_zero = jnp.where(lanes < ranks[step, 0, 0], v0[0, 0], zero)
    v_next = jnp.where(lanes < ranks[step, 0, 1], v1[0, 0], zero)
    m_zero = dg(v_zero, heads[...], 0, 0)
    m_next = dg(v_next, tails[...], 0, 0)
    weights = jnp.concatenate(
        [m_zero[:, :NRHS] + m_zero[:, NRHS:], m_next[:, :NRHS] + m_next[:, NRHS:]], axis=0
    )
    pair = jnp.concatenate([u0[0, 0], u1[0, 0]], axis=1)
    all_lanes = lax.broadcasted_iota(jnp.int32, label_cols.shape, 1)
    mark = jnp.sum(jnp.where(all_lanes == step, label_cols[...], 0.0), axis=1, keepdims=True)
    out[0, 0] = onehot(mark) - mm_right(pair, weights)

    @pl.when(jnp.logical_and(step == 0, place[0] < 2))
    def _():
        out[0, 0] = lead[place[0]]

    @pl.when(step == pl.num_programs(0) - 1)
    def _():
        pltpu.make_async_copy(lowers, diag, sem).wait()


def local(coords, labels, ranks, u_first, v_first, u_second, v_second):
    position = lax.axis_index("row")
    cycles, _, height, rmax = u_first.shape
    number = lax.axis_size("row")
    whole = pl.BlockSpec(memory_space=pltpu.VMEM)
    smem = pl.BlockSpec(memory_space=pltpu.SMEM)
    lead_tile = pl.BlockSpec((1, 1, height, rmax), lambda i: (0, 0, 0, 0))
    square = jax.ShapeDtypeStruct((height, 2 * NRHS), BF16)
    lower_shape = jax.ShapeDtypeStruct((2, height, height), F32)
    heads, tails, lead, lowers = pl.pallas_call(
        first_kernel,
        grid=(1,),
        out_shape=(
            square, square, jax.ShapeDtypeStruct((2, height, NRHS), F32), lower_shape,
        ),
        in_specs=[smem, whole, whole, lead_tile, lead_tile],
        out_specs=(whole,) * 4,
        scratch_shapes=[
            pltpu.VMEM((height, 2 * height), F32),
            pltpu.VMEM((height, 2 * height), F32),
            pltpu.VMEM((NB, NB), F32),
            pltpu.VMEM((NB, NB), F32),
            pltpu.VMEM((2 * height, rmax), BF16),
            pltpu.VMEM((2, 1, height), jnp.int32),
            pltpu.SemaphoreType.DMA((number,)),
            pltpu.SemaphoreType.DMA,
            pltpu.SemaphoreType.DMA((number,)),
            pltpu.SemaphoreType.DMA((number,)),
            pltpu.SemaphoreType.DMA((number,)),
            pltpu.SemaphoreType.DMA((2,)),
        ],
        compiler_params=pltpu.CompilerParams(
            vmem_limit_bytes=VMEM_BYTES, collective_id=0, has_side_effects=True
        ),
        name="both_factors",
    )(ranks, coords, labels, u_first, v_first)

    tile = lambda width: pl.BlockSpec((1, 1, height, width), lambda i: (i, 0, 0, 0))
    return pl.pallas_call(
        second_kernel,
        grid=(cycles,),
        out_shape=(jax.ShapeDtypeStruct((cycles, 1, height, NRHS), F32), lower_shape),
        in_specs=[smem, smem, whole, whole, whole, whole, pl.BlockSpec(memory_space=pl.ANY)]
        + [tile(rmax)] * 4,
        out_specs=(tile(NRHS), pl.BlockSpec(memory_space=pl.ANY)),
        scratch_shapes=[pltpu.VMEM((height, 128), F32), pltpu.SemaphoreType.DMA],
        compiler_params=pltpu.CompilerParams(vmem_limit_bytes=VMEM_BYTES),
        name="tiles",
    )(
        position.reshape(1).astype(jnp.int32),
        ranks,
        labels,
        heads,
        tails,
        lead,
        lowers,
        u_first,
        v_first,
        u_second,
        v_second,
    )


def solution(mesh):
    in_specs = (
        P("parts", None, None),
        P("parts", "row", None),
        P("parts", "row", None),
        P("parts", "row", None, None),
        P("parts", "row", None, None),
        P("parts", "row", None, None),
        P("parts", "row", None, None),
    )
    out_specs = (P("parts", "row", None, None), P("parts", None, None))
    return jax.shard_map(local, mesh=mesh, in_specs=in_specs, out_specs=out_specs, check_vma=False)
```

time: 66.4 us -> 127 us (1.91)
  Pallas kernels: 57.8 us -> 123 us
  local copies, waits for them, and re-layouts: 7.28 us -> 2.66 us
    pallas_call x1, Pallas kernels: 32.1 us -> 67.3 us  [local(): pl.pallas_call(second_kernel, grid=(cycles,), out_shape=(jax.ShapeDtypeSt...]
    pallas_call x1, Pallas kernels: 25.7 us -> 55.6 us  [local(): pl.pallas_call(first_kernel, grid=(1,), out_shape=(square, square, jax.Sh...]
    unnamed x18 -> x2, local copies, waits for them, and re-layouts: 6.53 us -> 2.66 us
where the time goes in v3:
time: 127 us; the launch traced here: 126 us
  Pallas kernels  123 us (97%)
  local copies, waits for them, and re-layouts  2.66 us (2%)
    pallas_call x1, Pallas kernels, local(): pl.pallas_call(second_kernel, grid=(cycles,), out_shape=(jax.ShapeDtypeSt...  67.3 us
    pallas_call x1, Pallas kernels, local(): pl.pallas_call(first_kernel, grid=(1,), out_shape=(square, square, jax.Sh...  55.6 us
    unnamed x2, local copies, waits for them, and re-layouts  2.66 us

profile of v3, /device:TPU:0, one launch (start us, length us, event | category | flops | bytes accessed | tf_op | source)
XLA Modules:
  0.0 126.4 jit_solution(17717072206531971837)
XLA Ops:
  0.6 1.3 %copy.11.ranks = s32[8,1,2]{2,1,0:T(1,128)} copy(s32[8,1,2]{0,2,1:T(2,128)} %param.9) | data formatting | bytes 128 | tf_op args[2]
  2.0 1.3 %copy.10.coords = s32[2,3,512]{2,1,0:T(4,128)} copy(s32[2,3,512]{2,0,1:T(2,128)} %param.7) | data formatting | bytes 24576 | tf_op args[0]
  3.3 55.6 %both_factors.1 = (bf16[512,512]{1,0:T(8,128)(2,1)}, bf16[512,512]{1,0:T(8,128)(2,1)}, f32[2,512,256]{2,1,0:T(8,128)}, f32[2,512,512]{2,1,0:T(8,128)}) custom-call(s32[8,1,2]{2,1,0:T(1,128)} %copy.11.ranks, s32[2,3,512]{2,1,0:T(4,128)} %copy.10.coords, s32[8,1,512]{2,1,0:T(1,128)} %labels.3, bf16[8,1,512,128]{3,2,1,0:T(8,128)(2,1)} %u0.1, ...), custom_call_target="tpu_custom_call" | custom-call | tf_op jit(solution)/shard_map/both_factors/pallas_call | solution.py:341
  58.9 67.3 %tiles.1 = (f32[8,1,512,256]{3,2,1,0:T(8,128)}, f32[2,512,512]{2,1,0:T(8,128)}) custom-call(s32[1]{0:T(128)} %bitcast.place, s32[8,1,2]{2,1,0:T(1,128)} %copy.11.ranks, s32[8,1,512]{2,1,0:T(1,128)} %labels.3, bf16[512,512]{1,0:T(8,128)(2,1)} %get-tuple-element.6.heads, bf16[512,512]{1,0:T(8,128)(2,1)} %get-tuple-element.7.tails, ...), custom_call_target="tpu_custom_call" | custom-call | tf_op jit(solution)/shard_map/tiles/pallas_call | solution.py:370
